TPU v7x, 32 devices: a whole 2x2x4 slice. The times are simulated.
32 devices in a mesh: ctx: 8 (over z, y), tp: 4 (over x, core).
Axes of the slice: x: 2, y: 2, z: 4, core: 2. Of those that a mesh axis runs over, the one named last changes fastest.
Arguments:
- queries: bfloat16 [4096, 2048], P('ctx', 'tp'), may hold values from -7 to 7
- keys: bfloat16 [4096, 2048], P('ctx', 'tp'), may hold values from -6 to 6
- values: bfloat16 [4096, 2048], P('ctx', 'tp'), may hold values from -6 to 6
- doc_ids: int32 [32], replicated, may hold values from 0 to 3, never falling along the last dimension, each value on 1 to 20 neighbouring positions
- span_start: int32 [4], replicated, may hold values from 0 to 31, as said below
- span_end: int32 [4], replicated, may hold values from 1 to 32, as said below
- out_weight: bfloat16 [2048, 4096], P('tp'), may hold values from -0.125 to 0.125
Outputs:
- mixed: bfloat16 [4096, 4096], P(('ctx', 'tp'))
Inputs may be any that keep to these rules, and one draw needn't show every extreme that they name: `doc_ids`: each document occupies consecutive blocks. Spans are disjoint and in increasing order; span s covers blocks span_start[s] to span_end[s] - 1. span_end[s] - span_start[s] is 1 to 4.
All inputs are finite; a program needn't handle non-finite values.
Results may differ from a plain program's by a relative error of at most 0.012.
Values may be sent and summed in bfloat16 or wider, within the bound.
A program may use at most 128 MiB of HBM per device.

v0:
```python
import math

import jax
import jax.numpy as jnp
from jax import lax
from jax.sharding import PartitionSpec as P

HEAD_DIM = 128
BLOCK = 128


NEG = -1e30


def passed_along(value, axis, steps):
    count = lax.axis_size(axis)
    pairs = [(source, (source + steps) % count) for source in range(count)]
    return lax.ppermute(value, axis, pairs)


def block_spans(span_start, span_end, count):
    blocks = jnp.arange(count, dtype=jnp.int32)
    inside = (blocks[:, None] >= span_start[None, :]) & (blocks[:, None] < span_end[None, :])
    labels = jnp.arange(1, span_start.shape[0] + 1, dtype=jnp.int32)
    return jnp.sum(jnp.where(inside, labels[None, :], 0), axis=1) - 1


def token_labels(doc_ids, span_blocks, first, count):
    block_ids = (first + jnp.arange(count, dtype=jnp.int32)) // BLOCK
    onehot = block_ids[:, None] == jnp.arange(doc_ids.shape[0], dtype=jnp.int32)[None, :]
    docs = jnp.sum(jnp.where(onehot, doc_ids[None, :], 0), axis=1)
    spans = jnp.sum(jnp.where(onehot, span_blocks[None, :], 0), axis=1)
    return (docs, spans)


def per_device(queries, keys, values, doc_ids, span_start, span_end, out_weight):
    rows, local_width = queries.shape
    heads = local_width // HEAD_DIM
    own_index = lax.axis_index("ctx")
    n_ctx = lax.axis_size("ctx")
    scale = 1.0 / math.sqrt(HEAD_DIM)
    span_blocks = block_spans(span_start, span_end, doc_ids.shape[0])
    query_first = own_index * rows
    query_doc, query_span = token_labels(doc_ids, span_blocks, query_first, rows)
    query_pos = query_first + jnp.arange(rows, dtype=jnp.int32)
    query_heads = queries.reshape(rows, heads, HEAD_DIM)

    def attend_block(state, key_block, value_block, key_first):
        count = key_block.shape[0]
        key_doc, key_span = token_labels(doc_ids, span_blocks, key_first, count)
        key_pos = key_first + jnp.arange(count, dtype=jnp.int32)
        allowed = (query_doc[:, None] == key_doc[None, :]) & (
            (key_pos[None, :] <= query_pos[:, None])
            | (query_span[:, None] == key_span[None, :]) & (query_span[:, None] >= 0)
        )

        def compute(current):
            row_max, row_total, accum = current
            scores = (
                jnp.einsum(
                    "qhd,khd->hqk",
                    query_heads,
                    key_block.reshape(count, heads, HEAD_DIM),
                    preferred_element_type=jnp.float32,
                )
                * scale
            )
            scores = jnp.where(allowed[None], scores, NEG)
            new_max = jnp.maximum(row_max, jnp.max(scores, axis=2))
            weights = jnp.where(allowed[None], jnp.exp(scores - new_max[:, :, None]), 0.0)
            factor = jnp.exp(row_max - new_max)
            new_total = row_total * factor + jnp.sum(weights, axis=2)
            update = jnp.einsum(
                "hqk,khd->qhd",
                weights.astype(jnp.bfloat16),
                value_block.reshape(count, heads, HEAD_DIM),
                preferred_element_type=jnp.float32,
            )
            return (new_max, new_total, accum * factor.T[:, :, None] + update)

        return lax.cond(jnp.any(allowed), compute, lambda kept: kept, state)

    def attend_piece(state, key_piece, value_piece, key_first):
        count = key_piece.shape[0]
        return attend_block(state, key_piece, value_piece, key_first)

    initial = (
        jnp.full((heads, rows), NEG, jnp.float32),
        jnp.zeros((heads, rows), jnp.float32),
        jnp.zeros((rows, heads, HEAD_DIM), jnp.float32),
    )

    def pass_turn(turn, carry):
        state, key_now, value_now = carry
        source = (own_index - turn) % n_ctx
        state = attend_piece(state, key_now, value_now, source * rows)
        key_now, value_now = passed_along((key_now, value_now), "ctx", 1)
        return (state, key_now, value_now)

    state, key_last, value_last = lax.fori_loop(0, n_ctx - 1, pass_turn, (initial, keys, values))
    state = attend_piece(state, key_last, value_last, (own_index - (n_ctx - 1)) % n_ctx * rows)
    row_max, row_total, accum = state
    attended = (
        (accum / row_total.T[:, :, None]).reshape(rows, heads * HEAD_DIM).astype(jnp.bfloat16)
    )
    mixed = lax.psum_scatter(
        jnp.dot(attended, out_weight, preferred_element_type=jnp.float32).astype(jnp.bfloat16),
        "tp",
        scatter_dimension=0,
        tiled=True,
    )
    return mixed


def solution(mesh):
    return jax.shard_map(
        per_device,
        mesh=mesh,
        in_specs=(P("ctx", "tp"), P("ctx", "tp"), P("ctx", "tp"), P(), P(), P(), P("tp", None)),
        out_specs=P(("ctx", "tp"), None),
        check_vma=False,
    )
```

profile of v0, /device:TPU:25, one launch (start us, length us, event | category | flops | bytes accessed | tf_op | source)
XLA Modules:
  0.0 249.3 jit_solution(590310938443990143)
XLA Ops:
  6.6 0.8 select_reduce_fusion.6
  7.4 1.3 copy.30
  9.1 1.8 fusion.55
  11.7 168.7 %while.24 = (s32[]{:T(128)}, f32[4,512]{1,0:T(4,128)S(1)}, f32[4,512]{1,0:T(4,128)S(1)}, f32[512,4,128]{2,0,1:T(8,128)S(1)}, bf16[512,512]{1,0:T(8,128)(2,1)S(1)...) while((s32[]{:T(128)}, f32[4,512]{1,0:T(4,128)S(1)}, ...), condition=%wide.region_14.15_spmd.clone, body=%wide.region_6.14_spmd.clone.sunk | while | flops 552957952 | bytes 23752440 | solution.py:100
  11.7 0.8 copy.79
  12.5 1.2 collective-permute-start
  13.8 0.8 copy.80
  14.7 1.2 fusion.65
  16.5 5.9 %conditional.5 = ((f32[4,512]{1,0:T(4,128)S(1)}, f32[4,512]{1,0:T(4,128)S(1)}, f32[512,4,128]{2,0,1:T(8,128)S(1)})) conditional(s32[]{:T(128)} %convert_element_type.48, (f32[4,512]{1,0:T(4,128)S(1)}, f32[4,512]{1,0:T(4,128)S(1)}, f32[512,4,128]{2,0,1:T(8,128)S(1)}) %tuple.85, (pred[512,512]{0,1:T(8,128)(4,1)S(1)}, bf16[512,512]{1,0:T(8,128)(2,1)}, ...), branch_computations={%region_10.10_spmd, %region_11.13_spmd} | conditional | flops 551032832 | bytes 17170464 | solution.py:81
  16.6 1.9 fusion.2
  18.5 2.9 %fusion.11 = f32[512,4,128]{2,0,1:T(8,128)S(1)} fusion(f32[4,512,512]{1,2,0:T(8,128)S(1)} %get-tuple-element.517, f32[4,512]{1,0:T(4,128)S(1)} %get-tuple-element.626, pred[512,512]{0,1:T(8,128)(4,1)S(1)} %get-tuple-element.355, f32[512,4,128]{2,0,1:T(8,128)S(1)} %get-tuple-element.359, f32[512,4]{0,1:T(4,128)S(1)} %get-tuple-element.508, ...), kind=kOutput, calls=%fused_computation.9 | convolution fusion | flops 274202624 | bytes 7094272 | tf_op jit(solution)/shard_map/while/body/eval_jaxpr/cond/branch_1_fun/hqk,khd->qhd/dot_general | solution.py:73
  21.4 1.0 fusion.4
  22.5 4.0 %collective-permute-done = bf16[512,512]{1,0:T(8,128)(2,1)S(1)} collective-permute-done((bf16[512,512]{1,0:T(8,128)(2,1)}, bf16[512,512]{1,0:T(8,128)(2,1)S(1)}, u32[]{:S(2)}, u32[]{:S(2)}) %collective-permute-start) | collective-permute-done | bytes 524320 | tf_op jit(solution)/shard_map/while/body/eval_jaxpr/ppermute | solution.py:18
  26.4 11.2 %collective-permute-done.1 = bf16[512,512]{1,0:T(8,128)(2,1)S(1)} collective-permute-done((bf16[512,512]{1,0:T(8,128)(2,1)}, bf16[512,512]{1,0:T(8,128)(2,1)S(1)}, u32[]{:S(2)}, u32[]{:S(2)}) %collective-permute-start.1) | collective-permute-done | bytes 524320 | tf_op jit(solution)/shard_map/while/body/eval_jaxpr/ppermute | solution.py:18
  37.7 0.8 copy.79
  38.8 0.8 copy.80
  39.6 3.0 %collective-permute-start.1 = (bf16[512,512]{1,0:T(8,128)(2,1)}, bf16[512,512]{1,0:T(8,128)(2,1)S(1)}, u32[]{:S(2)}, u32[]{:S(2)}) collective-permute-start(bf16[512,512]{1,0:T(8,128)(2,1)} %copy.80), channel_id=1, source_target_pairs={{0,4},{4,8},{8,12},{12,16},{16,20},{20,24},{24,28},{28,0},{1,5},{5... | collective-permute-start | bytes 1572872 | tf_op jit(solution)/shard_map/while/body/eval_jaxpr/ppermute | solution.py:18
  42.8 1.2 fusion.65
  44.6 5.9 %conditional.5 = ((f32[4,512]{1,0:T(4,128)S(1)}, f32[4,512]{1,0:T(4,128)S(1)}, f32[512,4,128]{2,0,1:T(8,128)S(1)})) conditional(s32[]{:T(128)} %convert_element_type.48, (f32[4,512]{1,0:T(4,128)S(1)}, f32[4,512]{1,0:T(4,128)S(1)}, f32[512,4,128]{2,0,1:T(8,128)S(1)}) %tuple.85, (pred[512,512]{0,1:T(8,128)(4,1)S(1)}, bf16[512,512]{1,0:T(8,128)(2,1)}, ...), branch_computations={%region_10.10_spmd, %region_11.13_spmd} | conditional | flops 551032832 | bytes 17170464 | solution.py:81
  44.6 1.9 fusion.2
  46.6 2.9 %fusion.11 = f32[512,4,128]{2,0,1:T(8,128)S(1)} fusion(f32[4,512,512]{1,2,0:T(8,128)S(1)} %get-tuple-element.517, f32[4,512]{1,0:T(4,128)S(1)} %get-tuple-element.626, pred[512,512]{0,1:T(8,128)(4,1)S(1)} %get-tuple-element.355, f32[512,4,128]{2,0,1:T(8,128)S(1)} %get-tuple-element.359, f32[512,4]{0,1:T(4,128)S(1)} %get-tuple-element.508, ...), kind=kOutput, calls=%fused_computation.9 | convolution fusion | flops 274202624 | bytes 7094272 | tf_op jit(solution)/shard_map/while/body/eval_jaxpr/cond/branch_1_fun/hqk,khd->qhd/dot_general | solution.py:73
  49.4 1.0 fusion.4
  50.5 0.9 collective-permute-done
  51.4 11.2 %collective-permute-done.1 = bf16[512,512]{1,0:T(8,128)(2,1)S(1)} collective-permute-done((bf16[512,512]{1,0:T(8,128)(2,1)}, bf16[512,512]{1,0:T(8,128)(2,1)S(1)}, u32[]{:S(2)}, u32[]{:S(2)}) %collective-permute-start.1) | collective-permute-done | bytes 524320 | tf_op jit(solution)/shard_map/while/body/eval_jaxpr/ppermute | solution.py:18
  62.7 0.8 copy.79
  63.5 0.7 collective-permute-start
  64.2 0.8 copy.80
  65.0 4.8 %collective-permute-start.1 = (bf16[512,512]{1,0:T(8,128)(2,1)}, bf16[512,512]{1,0:T(8,128)(2,1)S(1)}, u32[]{:S(2)}, u32[]{:S(2)}) collective-permute-start(bf16[512,512]{1,0:T(8,128)(2,1)} %copy.80), channel_id=1, source_target_pairs={{0,4},{4,8},{8,12},{12,16},{16,20},{20,24},{24,28},{28,0},{1,5},{5... | collective-permute-start | bytes 1572872 | tf_op jit(solution)/shard_map/while/body/eval_jaxpr/ppermute | solution.py:18
  69.9 1.2 fusion.65
  71.7 5.9 %conditional.5 = ((f32[4,512]{1,0:T(4,128)S(1)}, f32[4,512]{1,0:T(4,128)S(1)}, f32[512,4,128]{2,0,1:T(8,128)S(1)})) conditional(s32[]{:T(128)} %convert_element_type.48, (f32[4,512]{1,0:T(4,128)S(1)}, f32[4,512]{1,0:T(4,128)S(1)}, f32[512,4,128]{2,0,1:T(8,128)S(1)}) %tuple.85, (pred[512,512]{0,1:T(8,128)(4,1)S(1)}, bf16[512,512]{1,0:T(8,128)(2,1)}, ...), branch_computations={%region_10.10_spmd, %region_11.13_spmd} | conditional | flops 551032832 | bytes 17170464 | solution.py:81
  71.7 1.9 fusion.2
  73.7 2.9 %fusion.11 = f32[512,4,128]{2,0,1:T(8,128)S(1)} fusion(f32[4,512,512]{1,2,0:T(8,128)S(1)} %get-tuple-element.517, f32[4,512]{1,0:T(4,128)S(1)} %get-tuple-element.626, pred[512,512]{0,1:T(8,128)(4,1)S(1)} %get-tuple-element.355, f32[512,4,128]{2,0,1:T(8,128)S(1)} %get-tuple-element.359, f32[512,4]{0,1:T(4,128)S(1)} %get-tuple-element.508, ...), kind=kOutput, calls=%fused_computation.9 | convolution fusion | flops 274202624 | bytes 7094272 | tf_op jit(solution)/shard_map/while/body/eval_jaxpr/cond/branch_1_fun/hqk,khd->qhd/dot_general | solution.py:73
  76.5 1.0 fusion.4
  77.6 9.1 %collective-permute-done.1 = bf16[512,512]{1,0:T(8,128)(2,1)S(1)} collective-permute-done((bf16[512,512]{1,0:T(8,128)(2,1)}, bf16[512,512]{1,0:T(8,128)(2,1)S(1)}, u32[]{:S(2)}, u32[]{:S(2)}) %collective-permute-start.1) | collective-permute-done | bytes 524320 | tf_op jit(solution)/shard_map/while/body/eval_jaxpr/ppermute | solution.py:18
  86.8 0.8 copy.79
  87.6 2.8 %collective-permute-start = (bf16[512,512]{1,0:T(8,128)(2,1)}, bf16[512,512]{1,0:T(8,128)(2,1)S(1)}, u32[]{:S(2)}, u32[]{:S(2)}) collective-permute-start(bf16[512,512]{1,0:T(8,128)(2,1)} %copy.79), channel_id=1, source_target_pairs={{0,4},{4,8},{8,12},{12,16},{16,20},{20,24},{24,28},{28,0},{1,5},{5... | collective-permute-start | bytes 1572872 | tf_op jit(solution)/shard_map/while/body/eval_jaxpr/ppermute | solution.py:18
  90.4 0.8 copy.80
  91.2 4.8 %collective-permute-start.1 = (bf16[512,512]{1,0:T(8,128)(2,1)}, bf16[512,512]{1,0:T(8,128)(2,1)S(1)}, u32[]{:S(2)}, u32[]{:S(2)}) collective-permute-start(bf16[512,512]{1,0:T(8,128)(2,1)} %copy.80), channel_id=1, source_target_pairs={{0,4},{4,8},{8,12},{12,16},{16,20},{20,24},{24,28},{28,0},{1,5},{5... | collective-permute-start | bytes 1572872 | tf_op jit(solution)/shard_map/while/body/eval_jaxpr/ppermute | solution.py:18
  96.1 1.2 fusion.65
  97.9 5.9 %conditional.5 = ((f32[4,512]{1,0:T(4,128)S(1)}, f32[4,512]{1,0:T(4,128)S(1)}, f32[512,4,128]{2,0,1:T(8,128)S(1)})) conditional(s32[]{:T(128)} %convert_element_type.48, (f32[4,512]{1,0:T(4,128)S(1)}, f32[4,512]{1,0:T(4,128)S(1)}, f32[512,4,128]{2,0,1:T(8,128)S(1)}) %tuple.85, (pred[512,512]{0,1:T(8,128)(4,1)S(1)}, bf16[512,512]{1,0:T(8,128)(2,1)}, ...), branch_computations={%region_10.10_spmd, %region_11.13_spmd} | conditional | flops 551032832 | bytes 17170464 | solution.py:81
  97.9 1.9 fusion.2
  99.9 2.9 %fusion.11 = f32[512,4,128]{2,0,1:T(8,128)S(1)} fusion(f32[4,512,512]{1,2,0:T(8,128)S(1)} %get-tuple-element.517, f32[4,512]{1,0:T(4,128)S(1)} %get-tuple-element.626, pred[512,512]{0,1:T(8,128)(4,1)S(1)} %get-tuple-element.355, f32[512,4,128]{2,0,1:T(8,128)S(1)} %get-tuple-element.359, f32[512,4]{0,1:T(4,128)S(1)} %get-tuple-element.508, ...), kind=kOutput, calls=%fused_computation.9 | convolution fusion | flops 274202624 | bytes 7094272 | tf_op jit(solution)/shard_map/while/body/eval_jaxpr/cond/branch_1_fun/hqk,khd->qhd/dot_general | solution.py:73
  102.7 1.0 fusion.4
  103.8 6.2 %collective-permute-done.1 = bf16[512,512]{1,0:T(8,128)(2,1)S(1)} collective-permute-done((bf16[512,512]{1,0:T(8,128)(2,1)}, bf16[512,512]{1,0:T(8,128)(2,1)S(1)}, u32[]{:S(2)}, u32[]{:S(2)}) %collective-permute-start.1) | collective-permute-done | bytes 524320 | tf_op jit(solution)/shard_map/while/body/eval_jaxpr/ppermute | solution.py:18
  110.1 0.8 copy.79
  110.8 4.8 %collective-permute-start = (bf16[512,512]{1,0:T(8,128)(2,1)}, bf16[512,512]{1,0:T(8,128)(2,1)S(1)}, u32[]{:S(2)}, u32[]{:S(2)}) collective-permute-start(bf16[512,512]{1,0:T(8,128)(2,1)} %copy.79), channel_id=1, source_target_pairs={{0,4},{4,8},{8,12},{12,16},{16,20},{20,24},{24,28},{28,0},{1,5},{5... | collective-permute-start | bytes 1572872 | tf_op jit(solution)/shard_map/while/body/eval_jaxpr/ppermute | solution.py:18
  115.6 0.8 copy.80
  116.5 4.8 %collective-permute-start.1 = (bf16[512,512]{1,0:T(8,128)(2,1)}, bf16[512,512]{1,0:T(8,128)(2,1)S(1)}, u32[]{:S(2)}, u32[]{:S(2)}) collective-permute-start(bf16[512,512]{1,0:T(8,128)(2,1)} %copy.80), channel_id=1, source_target_pairs={{0,4},{4,8},{8,12},{12,16},{16,20},{20,24},{24,28},{28,0},{1,5},{5... | collective-permute-start | bytes 1572872 | tf_op jit(solution)/shard_map/while/body/eval_jaxpr/ppermute | solution.py:18
  121.4 1.2 fusion.65
  123.2 11.2 %collective-permute-done.1 = bf16[512,512]{1,0:T(8,128)(2,1)S(1)} collective-permute-done((bf16[512,512]{1,0:T(8,128)(2,1)}, bf16[512,512]{1,0:T(8,128)(2,1)S(1)}, u32[]{:S(2)}, u32[]{:S(2)}) %collective-permute-start.1) | collective-permute-done | bytes 524320 | tf_op jit(solution)/shard_map/while/body/eval_jaxpr/ppermute | solution.py:18
  134.4 0.8 copy.79
  135.2 4.8 %collective-permute-start = (bf16[512,512]{1,0:T(8,128)(2,1)}, bf16[512,512]{1,0:T(8,128)(2,1)S(1)}, u32[]{:S(2)}, u32[]{:S(2)}) collective-permute-start(bf16[512,512]{1,0:T(8,128)(2,1)} %copy.79), channel_id=1, source_target_pairs={{0,4},{4,8},{8,12},{12,16},{16,20},{20,24},{24,28},{28,0},{1,5},{5... | collective-permute-start | bytes 1572872 | tf_op jit(solution)/shard_map/while/body/eval_jaxpr/ppermute | solution.py:18
  140.0 0.8 copy.80
  140.8 4.8 %collective-permute-start.1 = (bf16[512,512]{1,0:T(8,128)(2,1)}, bf16[512,512]{1,0:T(8,128)(2,1)S(1)}, u32[]{:S(2)}, u32[]{:S(2)}) collective-permute-start(bf16[512,512]{1,0:T(8,128)(2,1)} %copy.80), channel_id=1, source_target_pairs={{0,4},{4,8},{8,12},{12,16},{16,20},{20,24},{24,28},{28,0},{1,5},{5... | collective-permute-start | bytes 1572872 | tf_op jit(solution)/shard_map/while/body/eval_jaxpr/ppermute | solution.py:18
  145.7 1.2 fusion.65
  147.6 10.3 %collective-permute-done.1 = bf16[512,512]{1,0:T(8,128)(2,1)S(1)} collective-permute-done((bf16[512,512]{1,0:T(8,128)(2,1)}, bf16[512,512]{1,0:T(8,128)(2,1)S(1)}, u32[]{:S(2)}, u32[]{:S(2)}) %collective-permute-start.1) | collective-permute-done | bytes 524320 | tf_op jit(solution)/shard_map/while/body/eval_jaxpr/ppermute | solution.py:18
  157.9 0.8 copy.79
  158.6 4.8 %collective-permute-start = (bf16[512,512]{1,0:T(8,128)(2,1)}, bf16[512,512]{1,0:T(8,128)(2,1)S(1)}, u32[]{:S(2)}, u32[]{:S(2)}) collective-permute-start(bf16[512,512]{1,0:T(8,128)(2,1)} %copy.79), channel_id=1, source_target_pairs={{0,4},{4,8},{8,12},{12,16},{16,20},{20,24},{24,28},{28,0},{1,5},{5... | collective-permute-start | bytes 1572872 | tf_op jit(solution)/shard_map/while/body/eval_jaxpr/ppermute | solution.py:18
  163.4 0.8 copy.80
  164.3 4.8 %collective-permute-start.1 = (bf16[512,512]{1,0:T(8,128)(2,1)}, bf16[512,512]{1,0:T(8,128)(2,1)S(1)}, u32[]{:S(2)}, u32[]{:S(2)}) collective-permute-start(bf16[512,512]{1,0:T(8,128)(2,1)} %copy.80), channel_id=1, source_target_pairs={{0,4},{4,8},{8,12},{12,16},{16,20},{20,24},{24,28},{28,0},{1,5},{5... | collective-permute-start | bytes 1572872 | tf_op jit(solution)/shard_map/while/body/eval_jaxpr/ppermute | solution.py:18
  169.2 1.2 fusion.65
  171.0 9.3 %collective-permute-done.1 = bf16[512,512]{1,0:T(8,128)(2,1)S(1)} collective-permute-done((bf16[512,512]{1,0:T(8,128)(2,1)}, bf16[512,512]{1,0:T(8,128)(2,1)S(1)}, u32[]{:S(2)}, u32[]{:S(2)}) %collective-permute-start.1) | collective-permute-done | bytes 524320 | tf_op jit(solution)/shard_map/while/body/eval_jaxpr/ppermute | solution.py:18
  180.9 6.5 %convolution_convert_fusion = bf16[512,4096]{1,0:T(8,128)(2,1)} fusion(bf16[512,512]{0,1:T(8,128)(2,1)S(1)} %bitcast.51, bf16[512,4096]{1,0:T(8,128)(2,1)} %param.19), kind=kOutput, calls=%fused_computation.56 | convolution fusion | flops 2149580800 | bytes 8912896 | tf_op jit(solution)/shard_map/dot_general | solution.py:107
  187.4 55.1 %reduce-scatter.2.cloned.1.call-done = bf16[128,4096]{1,0:T(8,128)(2,1)} async-done(((bf16[512,4096]{1,0:T(8,128)(2,1)}), bf16[128,4096]{1,0:T(8,128)(2,1)}) %reduce-scatter.2.cloned.1.call-update) | async-done | bytes 1048592 | tf_op jit(solution)/shard_map/reduce_scatter | solution.py:106
  (73 shorter events, 2.7 us)
Async XLA Ops:
  6.5 5.2 %copy-start = (bf16[512,512]{1,0:T(8,128)(2,1)S(1)}, bf16[512,512]{1,0:T(8,128)(2,1)}, u32[]{:S(2)}) copy-start(bf16[512,512]{1,0:T(8,128)(2,1)} %param.14) | copy-start | bytes 1572868
  6.5 5.2 %copy-start.1 = (bf16[512,512]{1,0:T(8,128)(2,1)S(1)}, bf16[512,512]{1,0:T(8,128)(2,1)}, u32[]{:S(2)}) copy-start(bf16[512,512]{1,0:T(8,128)(2,1)} %param.15) | copy-start | bytes 1572868
  6.5 2.4 copy-start.4
  6.5 235.9 %reduce-scatter.2.cloned.1.call-start = ((), (), s32[]{:S(2)}) async-start(), calls=%async_computation.1 | async-start | bytes 5242880 | tf_op jit(solution)/shard_map/reduce_scatter | solution.py:106
  8.7 2.3 copy-start.2
  12.5 13.9 %collective-permute-start = (bf16[512,512]{1,0:T(8,128)(2,1)}, bf16[512,512]{1,0:T(8,128)(2,1)S(1)}, u32[]{:S(2)}, u32[]{:S(2)}) collective-permute-start(bf16[512,512]{1,0:T(8,128)(2,1)} %copy.79), channel_id=1, source_target_pairs={{0,4},{4,8},{8,12},{12,16},{16,20},{20,24},{24,28},{28,0},{1,5},{5... | collective-permute-start | bytes 1572872 | tf_op jit(solution)/shard_map/while/body/eval_jaxpr/ppermute | solution.py:18
  14.6 23.1 %collective-permute-start.1 = (bf16[512,512]{1,0:T(8,128)(2,1)}, bf16[512,512]{1,0:T(8,128)(2,1)S(1)}, u32[]{:S(2)}, u32[]{:S(2)}) collective-permute-start(bf16[512,512]{1,0:T(8,128)(2,1)} %copy.80), channel_id=1, source_target_pairs={{0,4},{4,8},{8,12},{12,16},{16,20},{20,24},{24,28},{28,0},{1,5},{5... | collective-permute-start | bytes 1572872 | tf_op jit(solution)/shard_map/while/body/eval_jaxpr/ppermute | solution.py:18
  38.5 13.0 %collective-permute-start = (bf16[512,512]{1,0:T(8,128)(2,1)}, bf16[512,512]{1,0:T(8,128)(2,1)S(1)}, u32[]{:S(2)}, u32[]{:S(2)}) collective-permute-start(bf16[512,512]{1,0:T(8,128)(2,1)} %copy.79), channel_id=1, source_target_pairs={{0,4},{4,8},{8,12},{12,16},{16,20},{20,24},{24,28},{28,0},{1,5},{5... | collective-permute-start | bytes 1572872 | tf_op jit(solution)/shard_map/while/body/eval_jaxpr/ppermute | solution.py:18
  39.6 23.1 %collective-permute-start.1 = (bf16[512,512]{1,0:T(8,128)(2,1)}, bf16[512,512]{1,0:T(8,128)(2,1)S(1)}, u32[]{:S(2)}, u32[]{:S(2)}) collective-permute-start(bf16[512,512]{1,0:T(8,128)(2,1)} %copy.80), channel_id=1, source_target_pairs={{0,4},{4,8},{8,12},{12,16},{16,20},{20,24},{24,28},{28,0},{1,5},{5... | collective-permute-start | bytes 1572872 | tf_op jit(solution)/shard_map/while/body/eval_jaxpr/ppermute | solution.py:18
  63.5 14.2 %collective-permute-start = (bf16[512,512]{1,0:T(8,128)(2,1)}, bf16[512,512]{1,0:T(8,128)(2,1)S(1)}, u32[]{:S(2)}, u32[]{:S(2)}) collective-permute-start(bf16[512,512]{1,0:T(8,128)(2,1)} %copy.79), channel_id=1, source_target_pairs={{0,4},{4,8},{8,12},{12,16},{16,20},{20,24},{24,28},{28,0},{1,5},{5... | collective-permute-start | bytes 1572872 | tf_op jit(solution)/shard_map/while/body/eval_jaxpr/ppermute | solution.py:18
  65.0 21.8 %collective-permute-start.1 = (bf16[512,512]{1,0:T(8,128)(2,1)}, bf16[512,512]{1,0:T(8,128)(2,1)S(1)}, u32[]{:S(2)}, u32[]{:S(2)}) collective-permute-start(bf16[512,512]{1,0:T(8,128)(2,1)} %copy.80), channel_id=1, source_target_pairs={{0,4},{4,8},{8,12},{12,16},{16,20},{20,24},{24,28},{28,0},{1,5},{5... | collective-permute-start | bytes 1572872 | tf_op jit(solution)/shard_map/while/body/eval_jaxpr/ppermute | solution.py:18
  87.6 16.3 %collective-permute-start = (bf16[512,512]{1,0:T(8,128)(2,1)}, bf16[512,512]{1,0:T(8,128)(2,1)S(1)}, u32[]{:S(2)}, u32[]{:S(2)}) collective-permute-start(bf16[512,512]{1,0:T(8,128)(2,1)} %copy.79), channel_id=1, source_target_pairs={{0,4},{4,8},{8,12},{12,16},{16,20},{20,24},{24,28},{28,0},{1,5},{5... | collective-permute-start | bytes 1572872 | tf_op jit(solution)/shard_map/while/body/eval_jaxpr/ppermute | solution.py:18
  91.2 18.9 %collective-permute-start.1 = (bf16[512,512]{1,0:T(8,128)(2,1)}, bf16[512,512]{1,0:T(8,128)(2,1)S(1)}, u32[]{:S(2)}, u32[]{:S(2)}) collective-permute-start(bf16[512,512]{1,0:T(8,128)(2,1)} %copy.80), channel_id=1, source_target_pairs={{0,4},{4,8},{8,12},{12,16},{16,20},{20,24},{24,28},{28,0},{1,5},{5... | collective-permute-start | bytes 1572872 | tf_op jit(solution)/shard_map/while/body/eval_jaxpr/ppermute | solution.py:18
  110.8 12.4 %collective-permute-start = (bf16[512,512]{1,0:T(8,128)(2,1)}, bf16[512,512]{1,0:T(8,128)(2,1)S(1)}, u32[]{:S(2)}, u32[]{:S(2)}) collective-permute-start(bf16[512,512]{1,0:T(8,128)(2,1)} %copy.79), channel_id=1, source_target_pairs={{0,4},{4,8},{8,12},{12,16},{16,20},{20,24},{24,28},{28,0},{1,5},{5... | collective-permute-start | bytes 1572872 | tf_op jit(solution)/shard_map/while/body/eval_jaxpr/ppermute | solution.py:18
  116.5 18.0 %collective-permute-start.1 = (bf16[512,512]{1,0:T(8,128)(2,1)}, bf16[512,512]{1,0:T(8,128)(2,1)S(1)}, u32[]{:S(2)}, u32[]{:S(2)}) collective-permute-start(bf16[512,512]{1,0:T(8,128)(2,1)} %copy.80), channel_id=1, source_target_pairs={{0,4},{4,8},{8,12},{12,16},{16,20},{20,24},{24,28},{28,0},{1,5},{5... | collective-permute-start | bytes 1572872 | tf_op jit(solution)/shard_map/while/body/eval_jaxpr/ppermute | solution.py:18
  135.2 12.4 %collective-permute-start = (bf16[512,512]{1,0:T(8,128)(2,1)}, bf16[512,512]{1,0:T(8,128)(2,1)S(1)}, u32[]{:S(2)}, u32[]{:S(2)}) collective-permute-start(bf16[512,512]{1,0:T(8,128)(2,1)} %copy.79), channel_id=1, source_target_pairs={{0,4},{4,8},{8,12},{12,16},{16,20},{20,24},{24,28},{28,0},{1,5},{5... | collective-permute-start | bytes 1572872 | tf_op jit(solution)/shard_map/while/body/eval_jaxpr/ppermute | solution.py:18
  140.8 17.0 %collective-permute-start.1 = (bf16[512,512]{1,0:T(8,128)(2,1)}, bf16[512,512]{1,0:T(8,128)(2,1)S(1)}, u32[]{:S(2)}, u32[]{:S(2)}) collective-permute-start(bf16[512,512]{1,0:T(8,128)(2,1)} %copy.80), channel_id=1, source_target_pairs={{0,4},{4,8},{8,12},{12,16},{16,20},{20,24},{24,28},{28,0},{1,5},{5... | collective-permute-start | bytes 1572872 | tf_op jit(solution)/shard_map/while/body/eval_jaxpr/ppermute | solution.py:18
  158.6 12.4 %collective-permute-start = (bf16[512,512]{1,0:T(8,128)(2,1)}, bf16[512,512]{1,0:T(8,128)(2,1)S(1)}, u32[]{:S(2)}, u32[]{:S(2)}) collective-permute-start(bf16[512,512]{1,0:T(8,128)(2,1)} %copy.79), channel_id=1, source_target_pairs={{0,4},{4,8},{8,12},{12,16},{16,20},{20,24},{24,28},{28,0},{1,5},{5... | collective-permute-start | bytes 1572872 | tf_op jit(solution)/shard_map/while/body/eval_jaxpr/ppermute | solution.py:18
  164.3 16.1 %collective-permute-start.1 = (bf16[512,512]{1,0:T(8,128)(2,1)}, bf16[512,512]{1,0:T(8,128)(2,1)S(1)}, u32[]{:S(2)}, u32[]{:S(2)}) collective-permute-start(bf16[512,512]{1,0:T(8,128)(2,1)} %copy.80), channel_id=1, source_target_pairs={{0,4},{4,8},{8,12},{12,16},{16,20},{20,24},{24,28},{28,0},{1,5},{5... | collective-permute-start | bytes 1572872 | tf_op jit(solution)/shard_map/while/body/eval_jaxpr/ppermute | solution.py:18
Sparse Core Ops, SparseCore 0:
  187.5 54.9 reduce-scatter.1
where the time goes:
time: 252 us; the launch traced here: 249 us
  waiting for transfers between devices  129 us (51%)
  starting transfers between devices  46.4 us (18%)
  matrix products  25.6 us (10%)
  other arithmetic  16.3 us (6%)
  between operations  14.2 us (6%)
  local copies, waits for them, and re-layouts  13.2 us (5%)
  loops' own time  4.99 us (2%)
    ppermute x14, waiting for transfers between devices, passed_along(): return lax.ppermute(value, axis, pairs)  73.6 us
    reduce_scatter x1, waiting for transfers between devices, per_device(): lax.psum_scatter(jnp.dot(attended, out_weight, preferred_element_type=jnp...  55.1 us
    ppermute x14, starting transfers between devices, passed_along(): return lax.ppermute(value, axis, pairs)  46.4 us
    dot_general x4, matrix products, compute(): jnp.einsum('hqk,khd->qhd', weights.astype(jnp.bfloat16), value_block.resh...  11.4 us
    while x14, local copies, waits for them, and re-layouts  11.2 us
    reduce_or x8, other arithmetic, attend_block(): return lax.cond(jnp.any(allowed), compute, lambda kept: kept, state)  10.1 us
    dot_general x4, matrix products, compute(): jnp.einsum('qhd,khd->hqk', query_heads, key_block.reshape(count, heads, H...  7.71 us
    dot_general x1, matrix products, per_device(): jnp.dot(attended, out_weight, preferred_element_type=jnp.float32)  6.49 us
  transfers between devices with their start and end apart: 15, of which 10 were waited for; matrix products, arithmetic and copies ran while one was open for 15% of the time, Pallas kernels for 0%

commit v1 on v0

v1 whole, which is shorter than its diff:
```python
import functools
import math

import jax
import jax.numpy as jnp
from jax import lax
from jax.experimental import pallas as pl
from jax.experimental.pallas import tpu as pltpu
from jax.sharding import PartitionSpec as P

HEAD_DIM = 128
BLOCK = 128
NEG = -1e30
FLOOR = -1e29
MESH = pl.DeviceIdType.MESH
TAIL = 8


def kernel(
    levels, reach, doc_ref, start_ref, end_ref, q_ref, k_ref, v_ref, w_ref, out_ref,
    qbuf, kbuf, vbuf, kla, vla, lim, limla, part, stat, acc_s, acc_r, st_s, st_r, att, attq,
    wbuf, pbuf, keep, send1, recv1, send2, recv2,
    bar_q_s, q_r, kv_s, kv_r, la_s, la_r, o_s, o_r, s_s, s_r, loc, wsem, e1s, e1r, e2s, e2r,
):
    heads = qbuf.shape[1]
    rows = qbuf.shape[2]
    nb = rows // BLOCK
    depth = qbuf.shape[0]
    nspan = start_ref.shape[0]
    me = lax.axis_index("ctx")
    tp = lax.axis_index("tp")
    r, c = me // 2, me % 2
    a, core = tp // 2, tp % 2
    most = (reach + 1 - c) // 2
    const = math.log2(math.e) / math.sqrt(HEAD_DIM)

    up, down, side = (me + 2, tp), (me - 2, tp), (me + 1 - 2 * c, tp)
    mate, across = (me, tp + 1 - 2 * core), (me, tp + 2 - 4 * a)
    has_up, has_down = r < levels - 1, r > 0
    gives = (c == 0) & (r > 0)
    takes = (c == 1) & (r < levels - 1)

    barrier = pltpu.get_barrier_semaphore()
    for other in (side, mate, across):
        pl.semaphore_signal(barrier, inc=1, device_id=other, device_id_type=MESH)
    for cond, other in ((has_up, up), (has_down, down), (gives, (me - 1, tp)), (takes, (me + 1, tp))):
        @pl.when(cond)
        def _(other=other):
            pl.semaphore_signal(barrier, inc=1, device_id=other, device_id_type=MESH)

    w_copy = pltpu.make_async_copy(w_ref, wbuf, wsem)

    def cols(h):
        return pl.ds(pl.multiple_of(h * HEAD_DIM, HEAD_DIM), HEAD_DIM)

    mine = pl.ds(pl.multiple_of(c * rows, rows), rows)
    look = kla.shape[1]

    def local(j, h):
        src = (q_ref.at[:, cols(h)], k_ref.at[:, cols(h)], v_ref.at[:, cols(h)])[j]
        dst = (qbuf.at[0, h], kbuf.at[h, mine], vbuf.at[h, mine])[j]
        return pltpu.make_async_copy(src, dst, loc.at[j, h])

    def remote(src, dst, ss, rs, dev):
        return pltpu.make_async_remote_copy(
            src_ref=src, dst_ref=dst, send_sem=ss, recv_sem=rs, device_id=dev, device_id_type=MESH
        )

    def k_side(h):
        return remote(k_ref.at[:, cols(h)], kbuf.at[h, mine], kv_s.at[0, h], kv_r.at[0, h], side)

    def v_side(h):
        return remote(v_ref.at[:, cols(h)], vbuf.at[h, mine], kv_s.at[1, h], kv_r.at[1, h], side)

    def k_look(h):
        return remote(
            k_ref.at[pl.ds(0, look), cols(h)], kla.at[h], la_s.at[0, h], la_r.at[0, h], (me - 1, tp)
        )

    def v_look(h):
        return remote(
            v_ref.at[pl.ds(0, look), cols(h)], vla.at[h], la_s.at[1, h], la_r.at[1, h], (me - 1, tp)
        )

    def q_own(h):
        return remote(q_ref.at[:, cols(h)], qbuf.at[1, h], bar_q_s.at[0, h], q_r.at[1, h], down)

    def q_pass(j, h):
        return remote(qbuf.at[j, h], qbuf.at[j + 1, h], bar_q_s.at[j, h], q_r.at[j + 1, h], down)

    def o_up(j, h):
        return remote(acc_s.at[j, h], acc_r.at[j - 1, h], o_s.at[j, h], o_r.at[j - 1, h], up)

    def s_up(j, h):
        return remote(st_s.at[j, h], st_r.at[j - 1, h], s_s.at[j, h], s_r.at[j - 1, h], up)

    def valid(j):
        return (r + j < levels) & (j <= most)

    def below(j):
        return has_down & (j + 1 <= most)

    @pl.loop(0, heads)
    def _(h):
        for j in range(3):
            local(j, h).start()

    w_copy.start()
    total = 3 + sum(x.astype(jnp.int32) for x in (has_up, has_down, gives, takes))
    pl.semaphore_wait(barrier, total)

    @pl.loop(0, heads)
    def _(h):
        k_side(h).start()

        @pl.when(below(0))
        def _():
            q_own(h).start()

        v_side(h).start()

        @pl.when(gives)
        def _():
            k_look(h).start()
            v_look(h).start()

    def span_of(b):
        total = jnp.int32(-1)
        for s in range(nspan):
            total = jnp.where((b >= start_ref[s]) & (b < end_ref[s]), jnp.int32(s), total)
        return total

    lane = lax.broadcasted_iota(jnp.int32, (1, rows), 1)

    def row_of(values):
        row = jnp.full((1, rows), values[0], jnp.int32)
        for n in range(1, nb):
            row = jnp.where(lane >= n * BLOCK, values[n], row)
        return row

    def limit(qdoc, qspan, qpos, kb):
        kd, ks = doc_ref[kb], span_of(kb)
        reachable = jnp.where((qspan == ks) & (qspan >= 0), BLOCK, qpos - kb * BLOCK)
        return jnp.where(qdoc == kd, reachable, -1)

    @pl.loop(0, depth)
    def _(j):
        @pl.when(valid(j))
        def _():
            qi = me + 2 * j
            qdoc = row_of([doc_ref[qi * nb + n] for n in range(nb)])
            qspan = row_of([span_of(qi * nb + n) for n in range(nb)])
            qpos = lane + qi * rows
            for n in range(2 * nb):
                lim[j, n] = limit(qdoc, qspan, qpos, 2 * r * nb + n)

            @pl.when((j == 0) & takes)
            def _():
                for n in range(look // BLOCK):
                    limla[n] = limit(qdoc, qspan, qpos, (me + 1) * nb + n)

    def piece(q, kmat, vmat, limits):
        s = lax.dot_general(kmat, q, (((1,), (1,)), ((), ())), preferred_element_type=jnp.float32)
        n = s.shape[0] // BLOCK
        s = s.reshape(n, BLOCK, rows)
        place = lax.broadcasted_iota(jnp.int32, (n, BLOCK, rows), 1)
        s = jnp.where(place <= limits, s, NEG)
        m = jnp.maximum(jnp.max(jnp.max(s, axis=0), axis=0, keepdims=True), FLOOR)
        p = jnp.exp2((s - m[None]) * const)
        l = jnp.sum(jnp.sum(p, axis=0), axis=0, keepdims=True)
        p = p.astype(jnp.bfloat16).reshape(n * BLOCK, rows)
        o = lax.dot_general(vmat, p, (((0,), (0,)), ((), ())), preferred_element_type=jnp.float32)
        return o, m, l

    def merge(j, h, o, m, l, scale_o):
        om, ol = stat[j, h, 0:1], stat[j, h, 1:2]
        top = jnp.maximum(m, om)
        f_new = jnp.exp2((m - top) * const)
        f_old = jnp.exp2((om - top) * const)
        part[j, h] = part[j, h] * f_old + o * (f_new * scale_o)
        stat[j, h, 0:1] = top
        stat[j, h, 1:2] = ol * f_old + l * f_new

    @pl.loop(0, heads + 1)
    def _(step):
        @pl.when(step < heads)
        def _():
            h = step

            @pl.loop(1, depth)
            def _(j):
                @pl.when(valid(j))
                def _():
                    remote(qbuf.at[j, h], qbuf.at[j, h], bar_q_s.at[j, h], q_r.at[j, h], up).wait_recv()

                    @pl.when(below(j))
                    def _():
                        q_pass(j, h).start()

            for j in range(3):
                local(j, h).wait()
            k_side(h).wait_recv()
            v_side(h).wait_recv()

            @pl.loop(0, depth)
            def _(j):
                @pl.when(valid(j))
                def _():
                    o, m, l = piece(qbuf[j, h], kbuf[h], vbuf[h], lim[j])
                    part[j, h] = o
                    stat[j, h, 0:1] = m
                    stat[j, h, 1:2] = l

            @pl.when(takes)
            def _():
                k_look(h).wait_recv()
                v_look(h).wait_recv()
                o, m, l = piece(qbuf[0, h], kla[h], vla[h], limla[...])
                merge(0, h, o, m, l, 1.0)

        hf = jnp.where(has_down, step - 1, step)

        @pl.when((hf >= 0) & (hf < heads))
        def _():
            @pl.loop(0, depth)
            def _(j):
                @pl.when(valid(j))
                def _():
                    @pl.when(below(j))
                    def _():
                        remote(acc_s.at[j, hf], acc_r.at[j, hf], o_s.at[j, hf], o_r.at[j, hf], down).wait_recv()
                        remote(st_s.at[j, hf], st_r.at[j, hf], s_s.at[j, hf], s_r.at[j, hf], down).wait_recv()
                        m, l = st_r[j, hf, 0:1], st_r[j, hf, 1:2]
                        merge(j, hf, acc_r[j, hf].astype(jnp.float32), m, l, l)

                    l = stat[j, hf, 1:2]
                    o = (part[j, hf] * (1.0 / jnp.where(l > 0.0, l, 1.0))).astype(jnp.bfloat16)

                    @pl.when(j == 0)
                    def _():
                        att[hf] = o

                    @pl.when(j > 0)
                    def _():
                        acc_s[j, hf] = o
                        st_s[j, hf] = stat[j, hf]
                        o_up(j, hf).start()
                        s_up(j, hf).start()

    w_copy.wait()
    attq[...] = att[...].reshape(heads * HEAD_DIM, rows).T
    wide = pbuf.shape[2]
    piece_rows = pbuf.shape[1]
    chunks = keep.shape[0]

    def to_mate(n):
        return remote(send1.at[n], recv1.at[n], e1s.at[n], e1r.at[n], mate)

    def to_across(n):
        return remote(send2.at[n], recv2.at[n], e2s.at[n], e2r.at[n], across)

    def span(n):
        return pl.ds(pl.multiple_of(n * wide, wide), wide)

    @pl.loop(0, chunks + 1)
    def _(step):
        @pl.when(step < chunks)
        def _():
            n = step
            full = jnp.dot(attq[...], wbuf[:, span(n)], preferred_element_type=jnp.float32)
            pbuf[...] = full.reshape(4, piece_rows, wide)
            for t in range(2):
                send1[n, t] = pbuf[2 * t + 1 - core].astype(jnp.bfloat16)
                keep[n, t] = pbuf[2 * t + core]
            to_mate(n).start()

        @pl.when(step > 0)
        def _():
            n = step - 1
            to_mate(n).wait_recv()
            far = keep[n, 1 - a] + recv1[n, 1 - a].astype(jnp.float32)
            send2[n] = far.astype(jnp.bfloat16)
            to_across(n).start()

    @pl.loop(0, chunks)
    def _(n):
        to_across(n).wait_recv()
        near = keep[n, a] + recv1[n, a].astype(jnp.float32) + recv2[n].astype(jnp.float32)
        out_ref[:, span(n)] = near.astype(out_ref.dtype)

    @pl.loop(0, chunks)
    def _(n):
        to_mate(n).wait_send()
        to_across(n).wait_send()

    @pl.loop(0, heads)
    def _(h):
        k_side(h).wait_send()
        v_side(h).wait_send()

        @pl.when(below(0))
        def _():
            q_own(h).wait_send()

        @pl.when(gives)
        def _():
            k_look(h).wait_send()
            v_look(h).wait_send()

        @pl.loop(1, depth)
        def _(j):
            @pl.when(valid(j))
            def _():
                o_up(j, h).wait_send()
                s_up(j, h).wait_send()

                @pl.when(below(j))
                def _():
                    q_pass(j, h).wait_send()


def solution(mesh):
    n_ctx, n_tp = mesh.shape["ctx"], mesh.shape["tp"]

    def per_device(queries, keys, values, doc_ids, span_start, span_end, out_weight):
        rows, width = queries.shape
        heads = width // HEAD_DIM
        blocks = doc_ids.shape[0]
        nb = rows // BLOCK
        longest = blocks * 5 // 8
        reach = min(-(-(longest - 1) // nb), n_ctx - 1)
        levels = n_ctx // 2
        depth = min((reach + 1) // 2, levels - 1) + 1
        model = out_weight.shape[1]
        chunks = TAIL
        wide = model // chunks
        piece = rows // n_tp
        bf, f32, i32 = jnp.bfloat16, jnp.float32, jnp.int32
        dma = pltpu.SemaphoreType.DMA
        look = 3 * BLOCK
        smem = pl.BlockSpec(memory_space=pltpu.SMEM)
        anym = pl.BlockSpec(memory_space=pl.ANY)
        flops = 4 * rows * rows * 2 * width * depth + 2 * rows * width * model
        return pl.pallas_call(
            functools.partial(kernel, levels, reach),
            out_shape=jax.ShapeDtypeStruct((piece, model), bf),
            in_specs=[smem, smem, smem, anym, anym, anym, anym],
            out_specs=pl.BlockSpec(memory_space=pltpu.VMEM),
            scratch_shapes=[
                pltpu.VMEM((depth, heads, rows, HEAD_DIM), bf),
                pltpu.VMEM((heads, 2 * rows, HEAD_DIM), bf),
                pltpu.VMEM((heads, 2 * rows, HEAD_DIM), bf),
                pltpu.VMEM((heads, look, HEAD_DIM), bf),
                pltpu.VMEM((heads, look, HEAD_DIM), bf),
                pltpu.VMEM((depth, 2 * nb, 1, rows), i32),
                pltpu.VMEM((3, 1, rows), i32),
                pltpu.VMEM((depth, heads, HEAD_DIM, rows), f32),
                pltpu.VMEM((depth, heads, 8, rows), f32),
                pltpu.VMEM((depth, heads, HEAD_DIM, rows), bf),
                pltpu.VMEM((depth, heads, HEAD_DIM, rows), bf),
                pltpu.VMEM((depth, heads, 8, rows), f32),
                pltpu.VMEM((depth, heads, 8, rows), f32),
                pltpu.VMEM((heads, HEAD_DIM, rows), bf),
                pltpu.VMEM((rows, width), bf),
                pltpu.VMEM(out_weight.shape, bf),
                pltpu.VMEM((4, piece, wide), f32),
                pltpu.VMEM((chunks, 2, piece, wide), f32),
                pltpu.VMEM((chunks, 2, piece, wide), bf),
                pltpu.VMEM((chunks, 2, piece, wide), bf),
                pltpu.VMEM((chunks, piece, wide), bf),
                pltpu.VMEM((chunks, piece, wide), bf),
                dma((depth, heads)), dma((depth, heads)),
                dma((2, heads)), dma((2, heads)),
                dma((2, heads)), dma((2, heads)),
                dma((depth, heads)), dma((depth, heads)),
                dma((depth, heads)), dma((depth, heads)),
                dma((3, heads)), dma,
                dma((chunks,)), dma((chunks,)),
                dma((chunks,)), dma((chunks,)),
            ],
            compiler_params=pltpu.CompilerParams(
                collective_id=0, has_side_effects=True, vmem_limit_bytes=60 * 1024 * 1024
            ),
            cost_estimate=pl.CostEstimate(
                flops=flops, bytes_accessed=8 * 1024 * 1024, transcendentals=0
            ),
        )(doc_ids, span_start, span_end, queries, keys, values, out_weight)

    return jax.shard_map(
        per_device,
        mesh=mesh,
        in_specs=(P("ctx", "tp"), P("ctx", "tp"), P("ctx", "tp"), P(), P(), P(), P("tp", None)),
        out_specs=P(("ctx", "tp"), None),
        check_vma=False,
    )
```

time: 252 us -> 135 us (0.54); the launches traced: 249 us -> 135 us
  Pallas kernels: 0 us -> 133 us
  waiting for transfers between devices: 129 us -> 0 us
  starting transfers between devices: 46.4 us -> 0 us
  matrix products: 25.6 us -> 0 us
  other arithmetic: 16.3 us -> 0 us
  between operations: 14.2 us -> 0.01 us
  local copies, waits for them, and re-layouts: 13.2 us -> 2.29 us
  loops' own time: 4.99 us -> 0 us
    pallas_call x0 -> x1, Pallas kernels: none -> 133 us  [per_device(): pl.pallas_call(functools.partial(kernel, levels, reach), out_shape=jax.Sh...]
    ppermute x14 -> x0, waiting for transfers between devices: 73.6 us -> none  [passed_along(): return lax.ppermute(value, axis, pairs)]
    reduce_scatter x1 -> x0, waiting for transfers between devices: 55.1 us -> none  [per_device(): lax.psum_scatter(jnp.dot(attended, out_weight, preferred_element_type=jnp...]
    ppermute x14 -> x0, starting transfers between devices: 46.4 us -> none  [passed_along(): return lax.ppermute(value, axis, pairs)]
    dot_general x9 -> x0, matrix products: 25.6 us -> none  [the longest x4 11.4 us: compute(): jnp.einsum('hqk,khd->qhd', weights.astype(jnp.bfloat16), value_block.resh...]
    while x14 -> x0, local copies, waits for them, and re-layouts: 11.2 us -> none
    reduce_or x8 -> x0, other arithmetic: 10.1 us -> none  [attend_block(): return lax.cond(jnp.any(allowed), compute, lambda kept: kept, state)]
    reduce_sum x13 -> x0, other arithmetic: 5.78 us -> none  [the longest x4 4.16 us: compute(): new_total = row_total * factor + jnp.sum(weights, axis=2)]
  transfers between devices with their start and end apart: 15 -> 0, of which waited for: 10 -> 0; matrix products, arithmetic and copies ran while one was open for 15% -> 0% of each run, Pallas kernels for 0% -> 0%
where the time goes in v1:
time: 135 us
  Pallas kernels  133 us (99%)
  local copies, waits for them, and re-layouts  2.29 us (2%)
    pallas_call x1, Pallas kernels, per_device(): pl.pallas_call(functools.partial(kernel, levels, reach), out_shape=jax.Sh...  133 us

profile of v1, /device:TPU:25, one launch (start us, length us, event | category | flops | bytes accessed | tf_op | source)
XLA Modules:
  0.0 134.9 jit_solution(480149889412390212)
XLA Ops:
  0.0 132.6 %shard_map.73 = bf16[128,4096]{1,0:T(8,128)(2,1)} custom-call(s32[32]{0:T(128)} %doc_ref.1, s32[4]{0:T(128)} %start_ref.1, s32[4]{0:T(128)} %end_ref.1, bf16[512,512]{1,0:T(8,128)(2,1)} %q_ref.1, bf16[512,512]{1,0:T(8,128)(2,1)} %k_ref.1, bf16[512,512]{1,0:T(8,128)(2,1)} %v_ref.1, bf16[512,4096]{1,0:T(8,128)(2,1)} %w_ref.1), custom_call_target="tpu_custom_call" | custom-call | flops 6442450944 | bytes 8388608 | tf_op jit(solution)/shard_map/pallas_call | solution.py:344
  132.6 2.3 %copy.9 = bf16[128,4096]{1,0:T(8,128)(2,1)} copy(bf16[128,4096]{1,0:T(8,128)(2,1)} %shard_map.73) | data formatting | bytes 2097152

commit v2 on v1

--- a/solution.py
+++ b/solution.py
@@ -19,7 +19,7 @@
 def kernel(
     levels, reach, doc_ref, start_ref, end_ref, q_ref, k_ref, v_ref, w_ref, out_ref,
     qbuf, kbuf, vbuf, kla, vla, lim, limla, part, stat, acc_s, acc_r, st_s, st_r, att, attq,
-    wbuf, pbuf, keep, send1, recv1, send2, recv2,
+    wbuf, pbuf, keep, send1, recv1, send2, recv2, sbuf, wts, vt,
     bar_q_s, q_r, kv_s, kv_r, la_s, la_r, o_s, o_r, s_s, s_r, loc, wsem, e1s, e1r, e2s, e2r,
 ):
     heads = qbuf.shape[1]
@@ -159,27 +159,47 @@
                 for n in range(look // BLOCK):
                     limla[n] = limit(qdoc, qspan, qpos, (me + 1) * nb + n)
 
-    def piece(q, kmat, vmat, limits):
-        s = lax.dot_general(kmat, q, (((1,), (1,)), ((), ())), preferred_element_type=jnp.float32)
-        n = s.shape[0] // BLOCK
-        s = s.reshape(n, BLOCK, rows)
-        place = lax.broadcasted_iota(jnp.int32, (n, BLOCK, rows), 1)
-        s = jnp.where(place <= limits, s, NEG)
-        m = jnp.maximum(jnp.max(jnp.max(s, axis=0), axis=0, keepdims=True), FLOOR)
-        p = jnp.exp2((s - m[None]) * const)
-        l = jnp.sum(jnp.sum(p, axis=0), axis=0, keepdims=True)
-        p = p.astype(jnp.bfloat16).reshape(n * BLOCK, rows)
-        o = lax.dot_general(vmat, p, (((0,), (0,)), ((), ())), preferred_element_type=jnp.float32)
-        return o, m, l
-
-    def merge(j, h, o, m, l, scale_o):
-        om, ol = stat[j, h, 0:1], stat[j, h, 1:2]
+    half = rows // 2
+
+    def piece(j, h, k_at, vt_at, lim_at, count):
+        for side_q in range(2):
+            lanes = slice(side_q * half, (side_q + 1) * half)
+            q = qbuf[j, h, lanes, :]
+            top = None
+            for n in range(count):
+                s = lax.dot_general(
+                    k_at(n), q, (((1,), (1,)), ((), ())), preferred_element_type=jnp.float32
+                )
+                place = lax.broadcasted_iota(jnp.int32, (BLOCK, half), 0)
+                s = jnp.where(place <= lim_at(n, lanes), s, NEG)
+                sbuf[n, :, lanes] = s
+                most_here = jnp.max(s.reshape(BLOCK // 8, 8, half), axis=0)
+                top = most_here if top is None else jnp.maximum(top, most_here)
+            m = jnp.maximum(jnp.max(top, axis=0, keepdims=True), FLOOR)
+            shift = m * const
+            total = jnp.zeros((8, half), jnp.float32)
+            for n in range(count):
+                p = jnp.exp2(sbuf[n, :, lanes] * const - shift)
+                total = total + jnp.sum(p.reshape(BLOCK // 8, 8, half), axis=0)
+                wts[n * BLOCK : (n + 1) * BLOCK, lanes] = p.astype(jnp.bfloat16)
+            l = jnp.sum(total, axis=0, keepdims=True)
+            o = jnp.dot(vt_at(), wts[: count * BLOCK, lanes], preferred_element_type=jnp.float32)
+            yield lanes, o, m, l
+
+    def merge(j, h, lanes, o, m, l, scale_o):
+        om, ol = stat[j, h, 0:1, lanes], stat[j, h, 1:2, lanes]
         top = jnp.maximum(m, om)
         f_new = jnp.exp2((m - top) * const)
         f_old = jnp.exp2((om - top) * const)
-        part[j, h] = part[j, h] * f_old + o * (f_new * scale_o)
-        stat[j, h, 0:1] = top
-        stat[j, h, 1:2] = ol * f_old + l * f_new
+        part[j, h, :, lanes] = part[j, h, :, lanes] * f_old + o * (f_new * scale_o)
+        stat[j, h, 0:1, lanes] = top
+        stat[j, h, 1:2, lanes] = ol * f_old + l * f_new
+
+    def put(j, h, results):
+        for lanes, o, m, l in results:
+            part[j, h, :, lanes] = o
+            stat[j, h, 0:1, lanes] = m
+            stat[j, h, 1:2, lanes] = l
 
     @pl.loop(0, heads + 1)
     def _(step):
@@ -202,21 +222,38 @@
             k_side(h).wait_recv()
             v_side(h).wait_recv()
 
+            vt[...] = vbuf[h].T
+
             @pl.loop(0, depth)
             def _(j):
-                @pl.when(valid(j))
+                far = 2 * j + c > reach
+
+                def block(first):
+                    return lambda n: kbuf[h, (first + n) * BLOCK : (first + n + 1) * BLOCK, :]
+
+                @pl.when(valid(j) & jnp.logical_not(far))
                 def _():
-                    o, m, l = piece(qbuf[j, h], kbuf[h], vbuf[h], lim[j])
-                    part[j, h] = o
-                    stat[j, h, 0:1] = m
-                    stat[j, h, 1:2] = l
+                    put(j, h, piece(
+                        j, h, block(0), lambda: vt[...], lambda n, lanes: lim[j, n, :, lanes], 2 * nb
+                    ))
+
+                @pl.when(valid(j) & far)
+                def _():
+                    put(j, h, piece(
+                        j, h, block(nb), lambda: vt[:, rows:],
+                        lambda n, lanes: lim[j, nb + n, :, lanes], nb
+                    ))
 
             @pl.when(takes)
             def _():
                 k_look(h).wait_recv()
                 v_look(h).wait_recv()
-                o, m, l = piece(qbuf[0, h], kla[h], vla[h], limla[...])
-                merge(0, h, o, m, l, 1.0)
+                vt[:, :look] = vla[h].T
+                for lanes, o, m, l in piece(
+                    0, h, lambda n: kla[h, n * BLOCK : (n + 1) * BLOCK, :], lambda: vt[:, :look],
+                    lambda n, lanes: limla[n, :, lanes], look // BLOCK
+                ):
+                    merge(0, h, lanes, o, m, l, 1.0)
 
         hf = jnp.where(has_down, step - 1, step)
 
@@ -231,7 +268,7 @@
                         remote(acc_s.at[j, hf], acc_r.at[j, hf], o_s.at[j, hf], o_r.at[j, hf], down).wait_recv()
                         remote(st_s.at[j, hf], st_r.at[j, hf], s_s.at[j, hf], s_r.at[j, hf], down).wait_recv()
                         m, l = st_r[j, hf, 0:1], st_r[j, hf, 1:2]
-                        merge(j, hf, acc_r[j, hf].astype(jnp.float32), m, l, l)
+                        merge(j, hf, slice(None), acc_r[j, hf].astype(jnp.float32), m, l, l)
 
                     l = stat[j, hf, 1:2]
                     o = (part[j, hf] * (1.0 / jnp.where(l > 0.0, l, 1.0))).astype(jnp.bfloat16)
@@ -369,6 +406,9 @@
                 pltpu.VMEM((chunks, 2, piece, wide), bf),
                 pltpu.VMEM((chunks, piece, wide), bf),
                 pltpu.VMEM((chunks, piece, wide), bf),
+                pltpu.VMEM((2 * nb, BLOCK, rows), f32),
+                pltpu.VMEM((2 * rows, rows), bf),
+                pltpu.VMEM((HEAD_DIM, 2 * rows), bf),
                 dma((depth, heads)), dma((depth, heads)),
                 dma((2, heads)), dma((2, heads)),
                 dma((2, heads)), dma((2, heads)),

time: 135 us -> 136 us (level)
  no operation moved by 1% of the time
where the time goes in v2:
time: 136 us
  Pallas kernels  134 us (99%)
  local copies, waits for them, and re-layouts  2.29 us (2%)
    pallas_call x1, Pallas kernels, per_device(): pl.pallas_call(functools.partial(kernel, levels, reach), out_shape=jax.Sh...  134 us

profile of v2, /device:TPU:25, one launch (start us, length us, event | category | flops | bytes accessed | tf_op | source)
XLA Modules:
  0.0 136.2 jit_solution(9188256155460304163)
XLA Ops:
  0.0 133.9 %shard_map.73 = bf16[128,4096]{1,0:T(8,128)(2,1)} custom-call(s32[32]{0:T(128)} %doc_ref.1, s32[4]{0:T(128)} %start_ref.1, s32[4]{0:T(128)} %end_ref.1, bf16[512,512]{1,0:T(8,128)(2,1)} %q_ref.1, bf16[512,512]{1,0:T(8,128)(2,1)} %k_ref.1, bf16[512,512]{1,0:T(8,128)(2,1)} %v_ref.1, bf16[512,4096]{1,0:T(8,128)(2,1)} %w_ref.1), custom_call_target="tpu_custom_call" | custom-call | flops 6442450944 | bytes 8388608 | tf_op jit(solution)/shard_map/pallas_call | solution.py:381
  134.0 2.3 %copy.9 = bf16[128,4096]{1,0:T(8,128)(2,1)} copy(bf16[128,4096]{1,0:T(8,128)(2,1)} %shard_map.73) | data formatting | bytes 2097152

commit v3 on v2

--- a/solution.py
+++ b/solution.py
@@ -113,16 +113,31 @@
     def _(h):
         k_side(h).start()
 
+        v_side(h).start()
+
+    def give_own(h):
         @pl.when(below(0))
         def _():
             q_own(h).start()
-
-        v_side(h).start()
 
         @pl.when(gives)
         def _():
             k_look(h).start()
             v_look(h).start()
+
+    def pass_on(h):
+        @pl.loop(1, depth)
+        def _(j):
+            @pl.when(valid(j))
+            def _():
+                remote(qbuf.at[j, h], qbuf.at[j, h], bar_q_s.at[j, h], q_r.at[j, h], up).wait_recv()
+
+                @pl.when(below(j))
+                def _():
+                    q_pass(j, h).start()
+
+    for h in range(min(2, heads)):
+        give_own(h)
 
     def span_of(b):
         total = jnp.int32(-1)
@@ -201,21 +216,14 @@
             stat[j, h, 0:1, lanes] = m
             stat[j, h, 1:2, lanes] = l
 
-    @pl.loop(0, heads + 1)
+    lag = 2
+    pass_on(0)
+
+    @pl.loop(0, heads + lag)
     def _(step):
         @pl.when(step < heads)
         def _():
             h = step
-
-            @pl.loop(1, depth)
-            def _(j):
-                @pl.when(valid(j))
-                def _():
-                    remote(qbuf.at[j, h], qbuf.at[j, h], bar_q_s.at[j, h], q_r.at[j, h], up).wait_recv()
-
-                    @pl.when(below(j))
-                    def _():
-                        q_pass(j, h).start()
 
             for j in range(3):
                 local(j, h).wait()
@@ -244,21 +252,29 @@
                         lambda n, lanes: lim[j, nb + n, :, lanes], nb
                     ))
 
+        @pl.when(step + 2 < heads)
+        def _():
+            give_own(step + 2)
+
+        @pl.when(step + 1 < heads)
+        def _():
+            pass_on(step + 1)
+
+        hf = jnp.where(has_down, step - lag, step)
+
+        @pl.when((hf >= 0) & (hf < heads))
+        def _():
             @pl.when(takes)
             def _():
-                k_look(h).wait_recv()
-                v_look(h).wait_recv()
-                vt[:, :look] = vla[h].T
+                k_look(hf).wait_recv()
+                v_look(hf).wait_recv()
+                vt[:, :look] = vla[hf].T
                 for lanes, o, m, l in piece(
-                    0, h, lambda n: kla[h, n * BLOCK : (n + 1) * BLOCK, :], lambda: vt[:, :look],
+                    0, hf, lambda n: kla[hf, n * BLOCK : (n + 1) * BLOCK, :], lambda: vt[:, :look],
                     lambda n, lanes: limla[n, :, lanes], look // BLOCK
                 ):
-                    merge(0, h, lanes, o, m, l, 1.0)
-
-        hf = jnp.where(has_down, step - 1, step)
-
-        @pl.when((hf >= 0) & (hf < heads))
-        def _():
+                    merge(0, hf, lanes, o, m, l, 1.0)
+
             @pl.loop(0, depth)
             def _(j):
                 @pl.when(valid(j))

time: 136 us -> 120 us (0.88)
  Pallas kernels: 134 us -> 118 us
    pallas_call x1, Pallas kernels: 134 us -> 118 us  [per_device(): pl.pallas_call(functools.partial(kernel, levels, reach), out_shape=jax.Sh...]
where the time goes in v3:
time: 120 us
  Pallas kernels  118 us (98%)
  local copies, waits for them, and re-layouts  2.29 us (2%)
    pallas_call x1, Pallas kernels, per_device(): pl.pallas_call(functools.partial(kernel, levels, reach), out_shape=jax.Sh...  118 us

profile of v3, /device:TPU:25, one launch (start us, length us, event | category | flops | bytes accessed | tf_op | source)
XLA Modules:
  0.0 120.0 jit_solution(12173065597221718674)
XLA Ops:
  0.0 117.7 %shard_map.73 = bf16[128,4096]{1,0:T(8,128)(2,1)} custom-call(s32[32]{0:T(128)} %doc_ref.1, s32[4]{0:T(128)} %start_ref.1, s32[4]{0:T(128)} %end_ref.1, bf16[512,512]{1,0:T(8,128)(2,1)} %q_ref.1, bf16[512,512]{1,0:T(8,128)(2,1)} %k_ref.1, bf16[512,512]{1,0:T(8,128)(2,1)} %v_ref.1, bf16[512,4096]{1,0:T(8,128)(2,1)} %w_ref.1), custom_call_target="tpu_custom_call" | custom-call | flops 6442450944 | bytes 8388608 | tf_op jit(solution)/shard_map/pallas_call | solution.py:397
  117.7 2.3 %copy.9 = bf16[128,4096]{1,0:T(8,128)(2,1)} copy(bf16[128,4096]{1,0:T(8,128)(2,1)} %shard_map.73) | data formatting | bytes 2097152

commit v4 on v3

--- a/solution.py
+++ b/solution.py
@@ -17,7 +17,7 @@
 
 
 def kernel(
-    levels, reach, doc_ref, start_ref, end_ref, q_ref, k_ref, v_ref, w_ref, out_ref,
+    levels, reach, ahead, doc_ref, start_ref, end_ref, q_ref, k_ref, v_ref, w_ref, out_ref,
     qbuf, kbuf, vbuf, kla, vla, lim, limla, part, stat, acc_s, acc_r, st_s, st_r, att, attq,
     wbuf, pbuf, keep, send1, recv1, send2, recv2, sbuf, wts, vt,
     bar_q_s, q_r, kv_s, kv_r, la_s, la_r, o_s, o_r, s_s, s_r, loc, wsem, e1s, e1r, e2s, e2r,
@@ -31,7 +31,7 @@
     tp = lax.axis_index("tp")
     r, c = me // 2, me % 2
     a, core = tp // 2, tp % 2
-    most = (reach + 1 - c) // 2
+    most = jnp.minimum((reach + 1 - c) // 2, depth - 1)
     const = math.log2(math.e) / math.sqrt(HEAD_DIM)
 
     up, down, side = (me + 2, tp), (me - 2, tp), (me + 1 - 2 * c, tp)
@@ -39,11 +39,14 @@
     has_up, has_down = r < levels - 1, r > 0
     gives = (c == 0) & (r > 0)
     takes = (c == 1) & (r < levels - 1)
+    greeted = ((has_up, up), (has_down, down))
+    if ahead:
+        greeted += ((gives, (me - 1, tp)), (takes, (me + 1, tp)))
 
     barrier = pltpu.get_barrier_semaphore()
     for other in (side, mate, across):
         pl.semaphore_signal(barrier, inc=1, device_id=other, device_id_type=MESH)
-    for cond, other in ((has_up, up), (has_down, down), (gives, (me - 1, tp)), (takes, (me + 1, tp))):
+    for cond, other in greeted:
         @pl.when(cond)
         def _(other=other):
             pl.semaphore_signal(barrier, inc=1, device_id=other, device_id_type=MESH)
@@ -106,7 +109,7 @@
             local(j, h).start()
 
     w_copy.start()
-    total = 3 + sum(x.astype(jnp.int32) for x in (has_up, has_down, gives, takes))
+    total = 3 + sum(x.astype(jnp.int32) for x, _ in greeted)
     pl.semaphore_wait(barrier, total)
 
     @pl.loop(0, heads)
@@ -120,10 +123,12 @@
         def _():
             q_own(h).start()
 
-        @pl.when(gives)
-        def _():
-            k_look(h).start()
-            v_look(h).start()
+        if ahead:
+
+            @pl.when(gives)
+            def _():
+                k_look(h).start()
+                v_look(h).start()
 
     def pass_on(h):
         @pl.loop(1, depth)
@@ -169,10 +174,12 @@
             for n in range(2 * nb):
                 lim[j, n] = limit(qdoc, qspan, qpos, 2 * r * nb + n)
 
-            @pl.when((j == 0) & takes)
-            def _():
-                for n in range(look // BLOCK):
-                    limla[n] = limit(qdoc, qspan, qpos, (me + 1) * nb + n)
+            if ahead:
+
+                @pl.when((j == 0) & takes)
+                def _():
+                    for n in range(look // BLOCK):
+                        limla[n] = limit(qdoc, qspan, qpos, (me + 1) * nb + n)
 
     half = rows // 2
 
@@ -245,12 +252,14 @@
                         j, h, block(0), lambda: vt[...], lambda n, lanes: lim[j, n, :, lanes], 2 * nb
                     ))
 
-                @pl.when(valid(j) & far)
-                def _():
-                    put(j, h, piece(
-                        j, h, block(nb), lambda: vt[:, rows:],
-                        lambda n, lanes: lim[j, nb + n, :, lanes], nb
-                    ))
+                if 2 * depth - 1 > reach:
+
+                    @pl.when(valid(j) & far)
+                    def _():
+                        put(j, h, piece(
+                            j, h, block(nb), lambda: vt[:, rows:],
+                            lambda n, lanes: lim[j, nb + n, :, lanes], nb
+                        ))
 
         @pl.when(step + 2 < heads)
         def _():
@@ -264,16 +273,18 @@
 
         @pl.when((hf >= 0) & (hf < heads))
         def _():
-            @pl.when(takes)
-            def _():
-                k_look(hf).wait_recv()
-                v_look(hf).wait_recv()
-                vt[:, :look] = vla[hf].T
-                for lanes, o, m, l in piece(
-                    0, hf, lambda n: kla[hf, n * BLOCK : (n + 1) * BLOCK, :], lambda: vt[:, :look],
-                    lambda n, lanes: limla[n, :, lanes], look // BLOCK
-                ):
-                    merge(0, hf, lanes, o, m, l, 1.0)
+            if ahead:
+
+                @pl.when(takes)
+                def _():
+                    k_look(hf).wait_recv()
+                    v_look(hf).wait_recv()
+                    vt[:, :look] = vla[hf].T
+                    for lanes, o, m, l in piece(
+                        0, hf, lambda n: kla[hf, n * BLOCK : (n + 1) * BLOCK, :], lambda: vt[:, :look],
+                        lambda n, lanes: limla[n, :, lanes], look // BLOCK
+                    ):
+                        merge(0, hf, lanes, o, m, l, 1.0)
 
             @pl.loop(0, depth)
             def _(j):
@@ -355,10 +366,12 @@
         def _():
             q_own(h).wait_send()
 
-        @pl.when(gives)
-        def _():
-            k_look(h).wait_send()
-            v_look(h).wait_send()
+        if ahead:
+
+            @pl.when(gives)
+            def _():
+                k_look(h).wait_send()
+                v_look(h).wait_send()
 
         @pl.loop(1, depth)
         def _(j):
@@ -394,53 +407,66 @@
         smem = pl.BlockSpec(memory_space=pltpu.SMEM)
         anym = pl.BlockSpec(memory_space=pl.ANY)
         flops = 4 * rows * rows * 2 * width * depth + 2 * rows * width * model
-        return pl.pallas_call(
-            functools.partial(kernel, levels, reach),
-            out_shape=jax.ShapeDtypeStruct((piece, model), bf),
-            in_specs=[smem, smem, smem, anym, anym, anym, anym],
-            out_specs=pl.BlockSpec(memory_space=pltpu.VMEM),
-            scratch_shapes=[
-                pltpu.VMEM((depth, heads, rows, HEAD_DIM), bf),
-                pltpu.VMEM((heads, 2 * rows, HEAD_DIM), bf),
-                pltpu.VMEM((heads, 2 * rows, HEAD_DIM), bf),
-                pltpu.VMEM((heads, look, HEAD_DIM), bf),
-                pltpu.VMEM((heads, look, HEAD_DIM), bf),
-                pltpu.VMEM((depth, 2 * nb, 1, rows), i32),
-                pltpu.VMEM((3, 1, rows), i32),
-                pltpu.VMEM((depth, heads, HEAD_DIM, rows), f32),
-                pltpu.VMEM((depth, heads, 8, rows), f32),
-                pltpu.VMEM((depth, heads, HEAD_DIM, rows), bf),
-                pltpu.VMEM((depth, heads, HEAD_DIM, rows), bf),
-                pltpu.VMEM((depth, heads, 8, rows), f32),
-                pltpu.VMEM((depth, heads, 8, rows), f32),
-                pltpu.VMEM((heads, HEAD_DIM, rows), bf),
-                pltpu.VMEM((rows, width), bf),
-                pltpu.VMEM(out_weight.shape, bf),
-                pltpu.VMEM((4, piece, wide), f32),
-                pltpu.VMEM((chunks, 2, piece, wide), f32),
-                pltpu.VMEM((chunks, 2, piece, wide), bf),
-                pltpu.VMEM((chunks, 2, piece, wide), bf),
-                pltpu.VMEM((chunks, piece, wide), bf),
-                pltpu.VMEM((chunks, piece, wide), bf),
-                pltpu.VMEM((2 * nb, BLOCK, rows), f32),
-                pltpu.VMEM((2 * rows, rows), bf),
-                pltpu.VMEM((HEAD_DIM, 2 * rows), bf),
-                dma((depth, heads)), dma((depth, heads)),
-                dma((2, heads)), dma((2, heads)),
-                dma((2, heads)), dma((2, heads)),
-                dma((depth, heads)), dma((depth, heads)),
-                dma((depth, heads)), dma((depth, heads)),
-                dma((3, heads)), dma,
-                dma((chunks,)), dma((chunks,)),
-                dma((chunks,)), dma((chunks,)),
-            ],
-            compiler_params=pltpu.CompilerParams(
-                collective_id=0, has_side_effects=True, vmem_limit_bytes=60 * 1024 * 1024
-            ),
-            cost_estimate=pl.CostEstimate(
-                flops=flops, bytes_accessed=8 * 1024 * 1024, transcendentals=0
-            ),
-        )(doc_ids, span_start, span_end, queries, keys, values, out_weight)
+        def attend(depth, ahead, ident):
+            return pl.pallas_call(
+                functools.partial(kernel, levels, reach, ahead),
+                out_shape=jax.ShapeDtypeStruct((piece, model), bf),
+                in_specs=[smem, smem, smem, anym, anym, anym, anym],
+                out_specs=pl.BlockSpec(memory_space=pltpu.VMEM),
+                scratch_shapes=[
+                    pltpu.VMEM((depth, heads, rows, HEAD_DIM), bf),
+                    pltpu.VMEM((heads, 2 * rows, HEAD_DIM), bf),
+                    pltpu.VMEM((heads, 2 * rows, HEAD_DIM), bf),
+                    pltpu.VMEM((heads, look, HEAD_DIM), bf),
+                    pltpu.VMEM((heads, look, HEAD_DIM), bf),
+                    pltpu.VMEM((depth, 2 * nb, 1, rows), i32),
+                    pltpu.VMEM((3, 1, rows), i32),
+                    pltpu.VMEM((depth, heads, HEAD_DIM, rows), f32),
+                    pltpu.VMEM((depth, heads, 8, rows), f32),
+                    pltpu.VMEM((depth, heads, HEAD_DIM, rows), bf),
+                    pltpu.VMEM((depth, heads, HEAD_DIM, rows), bf),
+                    pltpu.VMEM((depth, heads, 8, rows), f32),
+                    pltpu.VMEM((depth, heads, 8, rows), f32),
+                    pltpu.VMEM((heads, HEAD_DIM, rows), bf),
+                    pltpu.VMEM((rows, width), bf),
+                    pltpu.VMEM(out_weight.shape, bf),
+                    pltpu.VMEM((4, piece, wide), f32),
+                    pltpu.VMEM((chunks, 2, piece, wide), f32),
+                    pltpu.VMEM((chunks, 2, piece, wide), bf),
+                    pltpu.VMEM((chunks, 2, piece, wide), bf),
+                    pltpu.VMEM((chunks, piece, wide), bf),
+                    pltpu.VMEM((chunks, piece, wide), bf),
+                    pltpu.VMEM((2 * nb, BLOCK, rows), f32),
+                    pltpu.VMEM((2 * rows, rows), bf),
+                    pltpu.VMEM((HEAD_DIM, 2 * rows), bf),
+                    dma((depth, heads)), dma((depth, heads)),
+                    dma((2, heads)), dma((2, heads)),
+                    dma((2, heads)), dma((2, heads)),
+                    dma((depth, heads)), dma((depth, heads)),
+                    dma((depth, heads)), dma((depth, heads)),
+                    dma((3, heads)), dma,
+                    dma((chunks,)), dma((chunks,)),
+                    dma((chunks,)), dma((chunks,)),
+                ],
+                compiler_params=pltpu.CompilerParams(
+                    collective_id=ident, has_side_effects=True, vmem_limit_bytes=60 * 1024 * 1024
+                ),
+                cost_estimate=pl.CostEstimate(
+                    flops=flops, bytes_accessed=8 * 1024 * 1024, transcendentals=0
+                ),
+            )
+
+        level = jnp.arange(blocks, dtype=jnp.int32) // (2 * nb)
+        same = doc_ids[:, None] == doc_ids[None, :]
+        farthest = jnp.max(jnp.where(same, level[:, None] - level[None, :], 0))
+        crossing = jnp.any(span_start // (2 * nb) != (span_end - 1) // (2 * nb))
+        which = jnp.where(crossing, 0, jnp.where(farthest < depth - 1, 2, 1))
+        return lax.switch(
+            which,
+            [attend(depth, True, 0), attend(depth, False, 1), attend(max(depth - 1, 1), False, 2)],
+            doc_ids, span_start, span_end, queries, keys, values, out_weight,
+        )
+
 
     return jax.shard_map(
         per_device,

time: 120 us -> 94.9 us (0.79); the launches traced: 120 us -> 93.6 us
  Pallas kernels: 118 us -> 88.4 us
  other arithmetic: 0 us -> 2.84 us
  between operations: 0.01 us -> 1.36 us
  local copies, waits for them, and re-layouts: 2.29 us -> 0.97 us
    pallas_call x1, Pallas kernels: 118 us -> 88.4 us  [per_device(): lax.switch(which, [attend(depth, True, 0), attend(depth, False, 1), atten...]
    reduce_max x0 -> x1, other arithmetic: none -> 1.52 us  [per_device(): farthest = jnp.max(jnp.where(same, level[:, None] - level[None, :], 0))]
    reduce_or x0 -> x1, other arithmetic: none -> 1.32 us  [per_device(): crossing = jnp.any(span_start // (2 * nb) != (span_end - 1) // (2 * nb))]
    unnamed x1, local copies, waits for them, and re-layouts: 2.29 us -> 0.97 us
where the time goes in v4:
time: 94.9 us; the launch traced here: 93.6 us
  Pallas kernels  88.4 us (93%)
  other arithmetic  2.84 us (3%)
  between operations  1.36 us (1%)
  local copies, waits for them, and re-layouts  0.97 us (1%)
    pallas_call x1, Pallas kernels, per_device(): lax.switch(which, [attend(depth, True, 0), attend(depth, False, 1), atten...  88.4 us

profile of v4, /device:TPU:25, one launch (start us, length us, event | category | flops | bytes accessed | tf_op | source)
XLA Modules:
  0.0 93.6 jit_solution(16474502244607599822)
XLA Ops:
  0.0 1.3 %compare_reduce_fusion = pred[]{:T(512)} fusion(s32[4]{0:T(128)} %param.15, s32[4]{0:T(128)} %param.14), kind=kLoop, calls=%fused_computation.2 | loop fusion | flops 131 | bytes 33 | tf_op jit(solution)/shard_map/reduce_or | solution.py:462
  1.3 1.5 %select_reduce_fusion = s32[]{:T(128)} fusion(s32[32]{0:T(128)S(1)} %and_select_fusion, s32[32]{0:T(128)} %param.13), kind=kLoop, calls=%fused_computation | loop fusion | flops 4095 | bytes 260 | tf_op jit(solution)/shard_map/reduce_max | solution.py:461
  4.2 88.4 %conditional.1 = (bf16[128,4096]{1,0:T(8,128)(2,1)S(1)}) conditional(s32[]{:T(128)} %clamp.3, (s32[32]{0:T(128)}, s32[4]{0:T(128)}, s32[4]{0:T(128)}, bf16[512,512]{1,0:T(8,128)(2,1)}, bf16[512,512]{1,0:T(8,128)(2,1)}, /*index=5*/bf16[512,512]{1,0:T(8,128)(2,1)}, bf16[512,4096]{1,0:T(8,128)(2,1)}) %tuple.14, (s32[32]{0:T(128)}, ...), branch_computations={%region_2.3_spmd, %region_3.4_spmd, %region_4.5_spmd} | conditional | flops 6442450944 | bytes 8388616 | solution.py:464
  4.2 88.4 %branch_2_fun.1 = bf16[128,4096]{1,0:T(8,128)(2,1)S(1)} custom-call(s32[32]{0:T(128)} %get-tuple-element.65.doc_ref, s32[4]{0:T(128)} %get-tuple-element.66.start_ref, s32[4]{0:T(128)} %get-tuple-element.67.end_ref, bf16[512,512]{1,0:T(8,128)(2,1)} %get-tuple-element.68.q_ref, bf16[512,512]{1,0:T(8,128)(2,1)} %get-tuple-element.69.k_ref, ...), custom_call_target="tpu_custom_call" | custom-call | flops 6442450944 | bytes 8388608 | tf_op jit(solution)/shard_map/cond/branch_2_fun/pallas_call | solution.py:464
  92.6 1.0 %copy.15 = bf16[128,4096]{1,0:T(8,128)(2,1)} copy(bf16[128,4096]{1,0:T(8,128)(2,1)S(1)} %get-tuple-element.72) | data formatting | bytes 2097152
  (1 shorter events, 0.0 us)

commit v5 on v4

--- a/solution.py
+++ b/solution.py
@@ -269,47 +269,47 @@
         def _():
             pass_on(step + 1)
 
-        hf = jnp.where(has_down, step - lag, step)
-
-        @pl.when((hf >= 0) & (hf < heads))
-        def _():
-            if ahead:
-
-                @pl.when(takes)
-                def _():
-                    k_look(hf).wait_recv()
-                    v_look(hf).wait_recv()
-                    vt[:, :look] = vla[hf].T
-                    for lanes, o, m, l in piece(
-                        0, hf, lambda n: kla[hf, n * BLOCK : (n + 1) * BLOCK, :], lambda: vt[:, :look],
-                        lambda n, lanes: limla[n, :, lanes], look // BLOCK
-                    ):
-                        merge(0, hf, lanes, o, m, l, 1.0)
-
-            @pl.loop(0, depth)
-            def _(j):
-                @pl.when(valid(j))
-                def _():
-                    @pl.when(below(j))
-                    def _():
-                        remote(acc_s.at[j, hf], acc_r.at[j, hf], o_s.at[j, hf], o_r.at[j, hf], down).wait_recv()
-                        remote(st_s.at[j, hf], st_r.at[j, hf], s_s.at[j, hf], s_r.at[j, hf], down).wait_recv()
-                        m, l = st_r[j, hf, 0:1], st_r[j, hf, 1:2]
-                        merge(j, hf, slice(None), acc_r[j, hf].astype(jnp.float32), m, l, l)
-
-                    l = stat[j, hf, 1:2]
-                    o = (part[j, hf] * (1.0 / jnp.where(l > 0.0, l, 1.0))).astype(jnp.bfloat16)
-
-                    @pl.when(j == 0)
-                    def _():
-                        att[hf] = o
-
-                    @pl.when(j > 0)
-                    def _():
-                        acc_s[j, hf] = o
-                        st_s[j, hf] = stat[j, hf]
-                        o_up(j, hf).start()
-                        s_up(j, hf).start()
+        if ahead:
+            hf = jnp.where(below(0), step - lag, step)
+
+            @pl.when(takes & (hf >= 0) & (hf < heads))
+            def _():
+                k_look(hf).wait_recv()
+                v_look(hf).wait_recv()
+                vt[:, :look] = vla[hf].T
+                for lanes, o, m, l in piece(
+                    0, hf, lambda n: kla[hf, n * BLOCK : (n + 1) * BLOCK, :], lambda: vt[:, :look],
+                    lambda n, lanes: limla[n, :, lanes], look // BLOCK
+                ):
+                    merge(0, hf, lanes, o, m, l, 1.0)
+
+        @pl.loop(0, depth)
+        def _(turn):
+            j = depth - 1 - turn
+            hf = jnp.where(below(j), step - lag, step)
+
+            @pl.when(valid(j) & (hf >= 0) & (hf < heads))
+            def _():
+                @pl.when(below(j))
+                def _():
+                    remote(acc_s.at[j, hf], acc_r.at[j, hf], o_s.at[j, hf], o_r.at[j, hf], down).wait_recv()
+                    remote(st_s.at[j, hf], st_r.at[j, hf], s_s.at[j, hf], s_r.at[j, hf], down).wait_recv()
+                    m, l = st_r[j, hf, 0:1], st_r[j, hf, 1:2]
+                    merge(j, hf, slice(None), acc_r[j, hf].astype(jnp.float32), m, l, l)
+
+                l = stat[j, hf, 1:2]
+                o = (part[j, hf] * (1.0 / jnp.where(l > 0.0, l, 1.0))).astype(jnp.bfloat16)
+
+                @pl.when(j == 0)
+                def _():
+                    att[hf] = o
+
+                @pl.when(j > 0)
+                def _():
+                    acc_s[j, hf] = o
+                    st_s[j, hf] = stat[j, hf]
+                    o_up(j, hf).start()
+                    s_up(j, hf).start()
 
     w_copy.wait()
     attq[...] = att[...].reshape(heads * HEAD_DIM, rows).T

time: 94.9 us -> 85.3 us (0.90)
  Pallas kernels: 88.4 us -> 79.1 us
    pallas_call x1, Pallas kernels: 88.4 us -> 79.1 us  [per_device(): lax.switch(which, [attend(depth, True, 0), attend(depth, False, 1), atten...]
where the time goes in v5:
time: 85.3 us; the launch traced here: 84.3 us
  Pallas kernels  79.1 us (93%)
  other arithmetic  2.84 us (3%)
  between operations  1.36 us (2%)
  local copies, waits for them, and re-layouts  0.97 us (1%)
    pallas_call x1, Pallas kernels, per_device(): lax.switch(which, [attend(depth, True, 0), attend(depth, False, 1), atten...  79.1 us

profile of v5, /device:TPU:25, one launch (start us, length us, event | category | flops | bytes accessed | tf_op | source)
XLA Modules:
  0.0 84.3 jit_solution(9574219715912102473)
XLA Ops:
  0.0 1.3 %compare_reduce_fusion = pred[]{:T(512)} fusion(s32[4]{0:T(128)} %param.15, s32[4]{0:T(128)} %param.14), kind=kLoop, calls=%fused_computation.2 | loop fusion | flops 131 | bytes 33 | tf_op jit(solution)/shard_map/reduce_or | solution.py:462
  1.3 1.5 %select_reduce_fusion = s32[]{:T(128)} fusion(s32[32]{0:T(128)S(1)} %and_select_fusion, s32[32]{0:T(128)} %param.13), kind=kLoop, calls=%fused_computation | loop fusion | flops 4095 | bytes 260 | tf_op jit(solution)/shard_map/reduce_max | solution.py:461
  4.2 79.2 %conditional.1 = (bf16[128,4096]{1,0:T(8,128)(2,1)S(1)}) conditional(s32[]{:T(128)} %clamp.3, (s32[32]{0:T(128)}, s32[4]{0:T(128)}, s32[4]{0:T(128)}, bf16[512,512]{1,0:T(8,128)(2,1)}, bf16[512,512]{1,0:T(8,128)(2,1)}, /*index=5*/bf16[512,512]{1,0:T(8,128)(2,1)}, bf16[512,4096]{1,0:T(8,128)(2,1)}) %tuple.14, (s32[32]{0:T(128)}, ...), branch_computations={%region_2.3_spmd, %region_3.4_spmd, %region_4.5_spmd} | conditional | flops 6442450944 | bytes 8388616 | solution.py:464
  4.2 79.1 %branch_2_fun.1 = bf16[128,4096]{1,0:T(8,128)(2,1)S(1)} custom-call(s32[32]{0:T(128)} %get-tuple-element.65.doc_ref, s32[4]{0:T(128)} %get-tuple-element.66.start_ref, s32[4]{0:T(128)} %get-tuple-element.67.end_ref, bf16[512,512]{1,0:T(8,128)(2,1)} %get-tuple-element.68.q_ref, bf16[512,512]{1,0:T(8,128)(2,1)} %get-tuple-element.69.k_ref, ...), custom_call_target="tpu_custom_call" | custom-call | flops 6442450944 | bytes 8388608 | tf_op jit(solution)/shard_map/cond/branch_2_fun/pallas_call | solution.py:464
  83.4 1.0 %copy.15 = bf16[128,4096]{1,0:T(8,128)(2,1)} copy(bf16[128,4096]{1,0:T(8,128)(2,1)S(1)} %get-tuple-element.72) | data formatting | bytes 2097152
  (1 shorter events, 0.0 us)
